TPU v7x, 512 devices: a whole 4x4x16 slice. The times are simulated.
512 devices in a mesh: dp: 16 (over z_lo, x), expert: 32 (over z_hi, y, core).
Axes of the slice: x: 4, y: 4, z: 16 (z_hi: 4, z_lo: 4; z = z_hi * 4 + z_lo), core: 2. Of those that a mesh axis runs over, the one named last changes fastest.
Arguments:
- tokens: bfloat16 [2048, 4096], P(('dp', 'expert')), may hold values from -6 to 6
- expert_ids: int32 [2048, 2], P(('dp', 'expert')), may hold values from 0 to 31, all different within a row; in each aligned block of 128 rows (0 to 127, 128 to 255, ...) at most 16 rows name the same one
- route_weights: bfloat16 [2048, 2], P(('dp', 'expert')), may hold values from 0.099609375 to 1
- out_grad: bfloat16 [2048, 4096], P(('dp', 'expert')), may hold values from -6 to 6
- gate_weight: bfloat16 [32, 1536, 4096], P('expert', 'dp'), may hold values from -0.09375 to 0.09375
- up_weight: bfloat16 [32, 1536, 4096], P('expert', 'dp'), may hold values from -0.09375 to 0.09375
- down_weight: bfloat16 [32, 1536, 4096], P('expert', 'dp'), may hold values from -0.15625 to 0.15625
Outputs:
- mixed: bfloat16 [2048, 4096], P(('dp', 'expert'))
- input_grad: bfloat16 [2048, 4096], P(('dp', 'expert'))
- gate_grad: bfloat16 [32, 1536, 4096], P('expert', 'dp')
- up_grad: bfloat16 [32, 1536, 4096], P('expert', 'dp')
- down_grad: bfloat16 [32, 1536, 4096], P('expert', 'dp')
Inputs may be any that keep to these rules, and one draw needn't show every extreme that they name: `expert_ids`: each row names 2 different experts. In each aligned block of 128 rows (the tokens of one index of dp) no expert is named by more than 16 rows, a bound that some block reaches.
All inputs are finite; a program needn't handle non-finite values.
Results may differ from a plain program's by a relative error of at most 0.024.
Values may be sent and summed in bfloat16 or wider, within the bound.
A program may use at most 64 MiB of HBM per device.

v0:
```python
import jax
import jax.numpy as jnp
from jax import lax
from jax.sharding import PartitionSpec as P

ROW_CAP = 16


def contract_rows(left, right):
    return lax.dot_general(
        left, right, (((1,), (1,)), ((), ())), preferred_element_type=jnp.float32
    )


def contract_first(left, right):
    return lax.dot_general(
        left, right, (((0,), (0,)), ((), ())), preferred_element_type=jnp.float32
    )


def shards(tokens, expert_ids, route_weights, out_grad, gate_weight, up_weight, down_weight):
    expert = lax.axis_index("expert")
    width = tokens.shape[1]
    local_tokens = tokens.shape[0]
    group_x, group_dy, group_w = (
        lax.all_gather(tokens, "expert", axis=0, tiled=True),
        lax.all_gather(out_grad, "expert", axis=0, tiled=True),
        lax.all_gather(route_weights, "expert", axis=0, tiled=True),
    )
    group_ids = lax.all_gather(expert_ids, "expert", axis=0, tiled=True)
    matches = group_ids == expert
    routed = jnp.any(matches, axis=1)
    weight = jnp.sum(jnp.where(matches, group_w.astype(jnp.float32), 0.0), axis=1)
    slot_rank = jnp.cumsum(routed.astype(jnp.int32)) - 1
    slot_index = jnp.arange(ROW_CAP, dtype=jnp.int32)
    picker = ((slot_rank[None, :] == slot_index[:, None]) & routed[None, :]).astype(jnp.bfloat16)
    slot_x = jnp.dot(picker, group_x, preferred_element_type=jnp.float32).astype(jnp.bfloat16)
    scaled = (weight[:, None] * group_dy.astype(jnp.float32)).astype(jnp.bfloat16)
    slot_dy = jnp.dot(picker, scaled, preferred_element_type=jnp.float32).astype(jnp.bfloat16)
    w_gate = gate_weight[0]
    w_up = up_weight[0]
    w_down = down_weight[0]
    all_x = lax.all_gather(slot_x, "dp", axis=0, tiled=True)
    gate_pre = contract_rows(w_gate, all_x)
    up_pre = contract_rows(w_up, all_x)
    gate_sig = jax.nn.sigmoid(gate_pre)
    silu_gate = gate_pre * gate_sig
    hidden = (silu_gate * up_pre).astype(jnp.bfloat16)
    expert_out = lax.psum_scatter(
        contract_first(hidden, w_down).astype(jnp.bfloat16), "dp", scatter_dimension=0, tiled=True
    )
    all_dy = lax.all_gather(slot_dy, "dp", axis=0, tiled=True)
    hidden_grad = contract_rows(w_down, all_dy)
    silu_slope = gate_sig * (1.0 + gate_pre * (1.0 - gate_sig))
    gate_act = (hidden_grad * up_pre * silu_slope).astype(jnp.bfloat16)
    up_act = (hidden_grad * silu_gate).astype(jnp.bfloat16)
    grad_down = jnp.dot(hidden, all_dy, preferred_element_type=jnp.float32).astype(jnp.bfloat16)
    grad_gate = jnp.dot(gate_act, all_x, preferred_element_type=jnp.float32).astype(jnp.bfloat16)
    grad_up = jnp.dot(up_act, all_x, preferred_element_type=jnp.float32).astype(jnp.bfloat16)
    expert_in = lax.psum_scatter(
        (contract_first(gate_act, w_gate) + contract_first(up_act, w_up)).astype(jnp.bfloat16),
        "dp",
        scatter_dimension=0,
        tiled=True,
    )
    back_out = contract_first(picker, expert_out).astype(jnp.bfloat16)
    back_in = contract_first(picker, expert_in).astype(jnp.bfloat16)
    got_out, got_in = (
        lax.all_to_all(back_out, "expert", split_axis=0, concat_axis=0, tiled=True),
        lax.all_to_all(back_in, "expert", split_axis=0, concat_axis=0, tiled=True),
    )
    expert_count = lax.axis_size("expert")
    got_out = got_out.reshape(expert_count, local_tokens, width)
    got_in = got_in.reshape(expert_count, local_tokens, width)
    expert_range = jnp.arange(expert_count, dtype=jnp.int32)
    own_match = expert_ids[:, :, None] == expert_range[None, None, :]
    mix_weight = jnp.sum(
        jnp.where(own_match, route_weights.astype(jnp.float32)[:, :, None], 0.0), axis=1
    )
    mixed_out = jnp.sum(jnp.transpose(mix_weight)[:, :, None] * got_out.astype(jnp.float32), axis=0)
    input_total = jnp.sum(got_in.astype(jnp.float32), axis=0)
    return (
        mixed_out.astype(jnp.bfloat16),
        input_total.astype(jnp.bfloat16),
        grad_gate[None],
        grad_up[None],
        grad_down[None],
    )


def solution(mesh):
    return jax.shard_map(
        shards,
        mesh=mesh,
        in_specs=(
            P(("dp", "expert"), None),
            P(("dp", "expert"), None),
            P(("dp", "expert"), None),
            P(("dp", "expert"), None),
            P("expert", "dp", None),
            P("expert", "dp", None),
            P("expert", "dp", None),
        ),
        out_specs=(
            P(("dp", "expert"), None),
            P(("dp", "expert"), None),
            P("expert", "dp", None),
            P("expert", "dp", None),
            P("expert", "dp", None),
        ),
        check_vma=False,
    )
```

profile of v0, /device:TPU:1, one launch (start us, length us, event | category | flops | bytes accessed | tf_op | source)
XLA Modules:
  0.0 613.2 jit_solution(17450783302044473673)
XLA Ops:
  7.2 0.0 copy-start
  7.2 0.0 copy-start.4
  7.2 0.0 all-gather.13.cloned.1.call-start
  7.2 0.7 all-gather.13.cloned.1.call-update
  7.9 0.0 all-gather.15.cloned.1.call-start
  8.0 0.7 all-gather.15.cloned.1.call-update
  8.7 0.0 all-gather.9.cloned.1.call-start
  8.7 60.9 %all-gather = s32[32,4,2]{1,2,0:T(2,128)S(1)} all-gather(s32[1,4,2]{1,2,0:T(2,128)} %bitcast.54), channel_id=1, replica_groups=mesh['dp'=16,'expert'=32] {'expert'}, dimensions={0}, use_global_device_ids=true | all-gather | bytes 1056 | tf_op jit(solution)/shard_map/all_gather | solution.py:30
  69.6 0.1 fusion.26
  69.7 0.1 reshape.68
  69.8 0.1 copy.22
  69.9 0.2 reduce-window.8
  70.1 0.1 add_reduce_fusion
  70.2 18.5 %all-gather.13.cloned.1.call-done = bf16[32,4,4096]{2,1,0:T(4,128)(2,1)} async-done(((bf16[1,4,4096]{2,1,0:T(4,128)(2,1)}), bf16[32,4,4096]{2,1,0:T(4,128)(2,1)}) %all-gather.13.cloned.1.call-update) | async-done | bytes 1048592 | tf_op jit(solution)/shard_map/all_gather | solution.py:26
  88.7 1.3 reshape.59
  90.0 0.9 convolution_convert_fusion.7
  90.9 0.0 all-gather.9.cloned.1.call-update
  90.9 0.0 all-gather.11.cloned.1.call-start
  91.0 0.0 copy-done.4
  91.0 51.2 %all-gather.2 = bf16[32,4,2]{1,2,0:T(2,128)(2,1)S(1)} all-gather(bf16[1,4,2]{1,2,0:T(2,128)(2,1)S(1)} %bitcast.55), channel_id=1, replica_groups=mesh['dp'=16,'expert'=32] {'expert'}, dimensions={0}, use_global_device_ids=true | all-gather | bytes 528 | tf_op jit(solution)/shard_map/all_gather | solution.py:28
  142.2 0.1 select_reduce_fusion
  142.3 0.1 reshape.71
  142.4 14.9 %all-gather.15.cloned.1.call-done = bf16[32,4,4096]{2,1,0:T(4,128)(2,1)} async-done(((bf16[1,4,4096]{2,1,0:T(4,128)(2,1)}), bf16[32,4,4096]{2,1,0:T(4,128)(2,1)}) %all-gather.15.cloned.1.call-update) | async-done | bytes 1048592 | tf_op jit(solution)/shard_map/all_gather | solution.py:27
  157.3 1.3 reshape.67
  158.6 1.0 convolution_convert_fusion.6
  159.6 0.0 all-gather.11.cloned.1.call-update
  159.6 0.0 reduce-scatter.3.cloned.1.call-start
  159.6 72.4 %all-gather.9.cloned.1.call-done = bf16[256,4096]{1,0:T(8,128)(2,1)} async-done(((bf16[16,4096]{1,0:T(8,128)(2,1)}), bf16[256,4096]{1,0:T(8,128)(2,1)}) %all-gather.9.cloned.1.call-update) | async-done | bytes 2097168 | tf_op jit(solution)/shard_map/all_gather | solution.py:43
  232.1 0.0 copy-start.1
  232.1 2.7 convolution_bitcast_fusion.1
  234.8 0.0 copy-done.1
  234.8 1.9 convolution_bitcast_fusion.2
  236.7 84.6 %all-gather.11.cloned.1.call-done = bf16[256,4096]{1,0:T(8,128)(2,1)} async-done(((bf16[16,4096]{1,0:T(8,128)(2,1)}), bf16[256,4096]{1,0:T(8,128)(2,1)}) %all-gather.11.cloned.1.call-update) | async-done | bytes 2097168 | tf_op jit(solution)/shard_map/all_gather | solution.py:52
  321.3 0.0 copy-done
  321.3 2.4 multiply_convert_fusion.2
  323.7 2.1 convolution_convert_fusion
  325.7 0.0 reduce-scatter.3.cloned.1.call-update
  325.7 0.0 reduce-scatter.5.cloned.1.call-start
  325.8 0.0 copy-start.2
  325.8 1.9 fusion.9
  327.7 0.0 copy-done.2
  327.8 2.0 fusion
  329.8 0.0 reduce-scatter.5.cloned.1.call-update
  329.8 86.0 %reduce-scatter.3.cloned.1.call-done = bf16[16,4096]{1,0:T(8,128)(2,1)} async-done(((bf16[256,4096]{1,0:T(8,128)(2,1)}), bf16[16,4096]{1,0:T(8,128)(2,1)}) %reduce-scatter.3.cloned.1.call-update) | async-done | bytes 131088 | tf_op jit(solution)/shard_map/reduce_scatter | solution.py:49
  415.8 2.4 convolution_convert_fusion.2
  418.2 2.2 all_to_all.12
  420.4 24.0 %all-to-all-start = ((bf16[32,4,4096]{2,1,0:T(4,128)(2,1)}), bf16[32,4,4096]{2,1,0:T(4,128)(2,1)}, u32[]{:S(2)}, u32[]{:S(2)}) async-start(bf16[32,4,4096]{2,1,0:T(4,128)(2,1)} %all_to_all.12), calls=%async_computation.1 | async-start | bytes 2097152 | tf_op jit(solution)/shard_map/all_to_all | solution.py:69
  444.5 85.5 %reduce-scatter.5.cloned.1.call-done = bf16[16,4096]{1,0:T(8,128)(2,1)} async-done(((bf16[256,4096]{1,0:T(8,128)(2,1)}), bf16[16,4096]{1,0:T(8,128)(2,1)}) %reduce-scatter.5.cloned.1.call-update) | async-done | bytes 131088 | tf_op jit(solution)/shard_map/reduce_scatter | solution.py:60
  530.0 2.4 convolution_convert_fusion.1
  532.4 0.0 copy-start.3
  532.4 2.3 all_to_all.14
  534.6 0.0 all-to-all-done
  534.6 21.5 %all-to-all-start.1 = ((bf16[32,4,4096]{2,1,0:T(4,128)(2,1)}), bf16[32,4,4096]{2,1,0:T(4,128)(2,1)}, u32[]{:S(2)}, u32[]{:S(2)}) async-start(bf16[32,4,4096]{2,1,0:T(4,128)(2,1)} %all_to_all.14), calls=%async_computation.3 | async-start | bytes 2097152 | tf_op jit(solution)/shard_map/all_to_all | solution.py:70
  556.1 0.0 copy-done.3
  556.1 0.1 select_reduce_fusion.1
  556.2 0.1 copy.21
  556.3 2.9 fusion.3
  559.3 1.4 fusion.2
  560.6 1.4 fusion.1
  562.0 2.5 multiply_reduce_fusion
  564.5 39.6 %all-to-all-done.1 = bf16[32,4,4096]{2,1,0:T(4,128)(2,1)} async-done(((bf16[32,4,4096]{2,1,0:T(4,128)(2,1)}), bf16[32,4,4096]{2,1,0:T(4,128)(2,1)}, u32[]{:S(2)}, u32[]{:S(2)}) %all-to-all-start.1) | async-done | bytes 1048608 | tf_op jit(solution)/shard_map/all_to_all | solution.py:70
  604.1 2.3 reduce_sum.42
  (2 shorter events, 0.0 us)
Async XLA Ops:
  7.2 314.1 %copy-start = (bf16[1,96,4096]{2,1,0:T(8,128)(2,1)S(1)}, bf16[1,96,4096]{2,1,0:T(8,128)(2,1)}, u32[]{:S(2)}) copy-start(bf16[1,96,4096]{2,1,0:T(8,128)(2,1)} %param.13) | copy-start | bytes 2359300
  7.2 83.8 %copy-start.4 = (bf16[4,2]{0,1:T(2,128)(2,1)S(1)}, bf16[4,2]{0,1:T(2,128)(2,1)}, u32[]{:S(2)}) copy-start(bf16[4,2]{0,1:T(2,128)(2,1)} %param.9) | copy-start | bytes 52
  7.2 81.5 %all-gather.13.cloned.1.call-start = ((), (), s32[]{:S(2)}) async-start(), calls=%async_computation.8 | async-start | bytes 1081344 | tf_op jit(solution)/shard_map/all_gather | solution.py:26
  7.9 149.4 %all-gather.15.cloned.1.call-start = ((), (), s32[]{:S(2)}) async-start(), calls=%async_computation.9 | async-start | bytes 1081344 | tf_op jit(solution)/shard_map/all_gather | solution.py:27
  8.7 223.4 %all-gather.9.cloned.1.call-start = ((), (), s32[]{:S(2)}) async-start(), calls=%async_computation.4 | async-start | bytes 2228224 | tf_op jit(solution)/shard_map/all_gather | solution.py:43
  90.9 230.3 %all-gather.11.cloned.1.call-start = ((), (), s32[]{:S(2)}) async-start(), calls=%async_computation.6 | async-start | bytes 2228224 | tf_op jit(solution)/shard_map/all_gather | solution.py:52
  159.6 256.3 %reduce-scatter.3.cloned.1.call-start = ((), (), s32[]{:S(2)}) async-start(), calls=%async_computation.5 | async-start | bytes 2228224 | tf_op jit(solution)/shard_map/reduce_scatter | solution.py:49
  232.1 2.7 copy-start.1
  325.7 204.3 %reduce-scatter.5.cloned.1.call-start = ((), (), s32[]{:S(2)}) async-start(), calls=%async_computation.7 | async-start | bytes 2228224 | tf_op jit(solution)/shard_map/reduce_scatter | solution.py:60
  325.8 2.0 copy-start.2
  420.4 114.2 %all-to-all-start = ((bf16[32,4,4096]{2,1,0:T(4,128)(2,1)}), bf16[32,4,4096]{2,1,0:T(4,128)(2,1)}, u32[]{:S(2)}, u32[]{:S(2)}) async-start(bf16[32,4,4096]{2,1,0:T(4,128)(2,1)} %all_to_all.12), calls=%async_computation.1 | async-start | bytes 2097152 | tf_op jit(solution)/shard_map/all_to_all | solution.py:69
  532.4 23.8 %copy-start.3 = (s32[4,2]{0,1:T(2,128)S(1)}, s32[4,2]{0,1:T(2,128)}, u32[]{:S(2)}) copy-start(s32[4,2]{0,1:T(2,128)} %param.8) | copy-start | bytes 100
  534.6 69.5 %all-to-all-start.1 = ((bf16[32,4,4096]{2,1,0:T(4,128)(2,1)}), bf16[32,4,4096]{2,1,0:T(4,128)(2,1)}, u32[]{:S(2)}, u32[]{:S(2)}) async-start(bf16[32,4,4096]{2,1,0:T(4,128)(2,1)} %all_to_all.14), calls=%async_computation.3 | async-start | bytes 2097152 | tf_op jit(solution)/shard_map/all_to_all | solution.py:70
Sparse Core Ops, SparseCore 0:
  11.2 77.4 all-gather.12
  91.8 65.4 all-gather.14
  159.9 72.0 all-gather.8
  234.6 86.6 all-gather.10
  325.9 89.9 reduce-scatter.2
  418.5 111.4 reduce-scatter.4
where the time goes:
time: 614 us; the launch traced here: 613 us
  waiting for transfers between devices  403 us (66%)
  blocking collectives  112 us (18%)
  starting transfers between devices  45.7 us (7%)
  matrix products  25.3 us (4%)
  between operations  14.3 us (2%)
  local copies, waits for them, and re-layouts  7.57 us (1%)
    reduce_scatter x1, waiting for transfers between devices, shards(): lax.psum_scatter(contract_first(hidden, w_down).astype(jnp.bfloat16), 'dp...  86 us
    reduce_scatter x1, waiting for transfers between devices, shards(): lax.psum_scatter((contract_first(gate_act, w_gate) + contract_first(up_ac...  85.5 us
    all_gather x1, waiting for transfers between devices, shards(): all_dy = lax.all_gather(slot_dy, 'dp', axis=0, tiled=True)  84.6 us
    all_gather x1, waiting for transfers between devices, shards(): all_x = lax.all_gather(slot_x, 'dp', axis=0, tiled=True)  72.4 us
    all_gather x1, blocking collectives, shards(): group_ids = lax.all_gather(expert_ids, 'expert', axis=0, tiled=True)  60.9 us
    all_gather x1, blocking collectives, shards(): lax.all_gather(route_weights, 'expert', axis=0, tiled=True)  51.2 us
    all_to_all x1, waiting for transfers between devices, shards(): lax.all_to_all(back_in, 'expert', split_axis=0, concat_axis=0, tiled=True)  39.6 us
    all_to_all x1, starting transfers between devices, shards(): lax.all_to_all(back_out, 'expert', split_axis=0, concat_axis=0, tiled=True)  24 us
  transfers between devices with their start and end apart: 8, of which 7 were waited for; matrix products, arithmetic and copies ran while one was open for 4% of the time, Pallas kernels for 0%

commit v1 on v0

v1 whole, which is shorter than its diff:
```python
import functools

import jax
import jax.numpy as jnp
from jax import lax
from jax.experimental import pallas as pl
from jax.experimental.pallas import tpu as pltpu
from jax.sharding import PartitionSpec as P

SIZES = (4, 4, 4, 4, 2)
CHUNKS = 4
SLOTS = 16
META = 128
F32 = jnp.float32
BF16 = jnp.bfloat16
MESH = pl.DeviceIdType.MESH


def nt(left, right):
    return lax.dot_general(left, right, (((1,), (1,)), ((), ())), preferred_element_type=F32)


def iota(shape, dim):
    return lax.broadcasted_iota(jnp.int32, shape, dim)


def ones_where(mask):
    return jnp.where(mask, 1.0, 0.0).astype(F32)


class Comm:
    def __init__(self, send, recv):
        self.send, self.recv, self.count, self.sent = send, recv, 0, []

    def reserve(self, amount):
        at = self.count
        self.count += amount
        return at

    def start(self, src, dst, device, sem):
        copy = pltpu.make_async_remote_copy(
            src_ref=src, dst_ref=dst, send_sem=self.send.at[sem], recv_sem=self.recv.at[sem],
            device_id=device, device_id_type=MESH,
        )
        copy.start()
        self.sent.append(copy)

    def arrived(self, dst, device, sem):
        pltpu.make_async_remote_copy(
            src_ref=dst, dst_ref=dst, send_sem=self.send.at[sem], recv_sem=self.recv.at[sem],
            device_id=device, device_id_type=MESH,
        ).wait_recv()

    def drain(self):
        for copy in self.sent:
            copy.wait_send()


class RingGather:
    def __init__(self, comm, buf, index, size, device, turn):
        self.comm, self.buf, self.i, self.n, self.device = comm, buf, index, size, device
        self.d = 1 if turn % 2 == 0 else -1
        self.sem = comm.reserve(3) if size > 1 else 0

    def at(self, step):
        return lax.rem(self.i + step + self.n, self.n)

    def near(self):
        if self.n == 1:
            return
        for j, step in enumerate((self.d, -self.d)):
            self.comm.start(self.buf.at[self.i], self.buf.at[self.i], self.device(self.at(step)), self.sem + j)

    def far(self):
        if self.n == 1:
            return
        back, ahead = self.at(-self.d), self.at(self.d)
        self.comm.arrived(self.buf.at[back], self.device(back), self.sem)
        self.comm.start(self.buf.at[back], self.buf.at[back], self.device(ahead), self.sem + 2)

    def finish(self):
        if self.n == 1:
            return
        ahead = self.at(self.d)
        self.comm.arrived(self.buf.at[ahead], self.device(ahead), self.sem + 1)
        self.comm.arrived(self.buf.at[self.at(2)], self.device(self.at(-self.d)), self.sem + 2)


class RingReduce:
    def __init__(self, comm, buf, far_buf, near_buf, index, size, device, turn):
        self.comm, self.buf, self.far_buf, self.near_buf = comm, buf, far_buf, near_buf
        self.i, self.n, self.device = index, size, device
        self.d = 1 if turn % 2 == 0 else -1
        self.sem = comm.reserve(3) if size > 1 else 0

    def at(self, step):
        return lax.rem(self.i + step + self.n, self.n)

    def first(self):
        if self.n == 1:
            return
        ahead, back = self.at(self.d), self.at(-self.d)
        self.comm.start(self.buf.at[self.at(2)], self.far_buf, self.device(ahead), self.sem)
        self.comm.start(self.buf.at[back], self.near_buf.at[1], self.device(back), self.sem + 1)

    def second(self):
        if self.n == 1:
            return
        ahead, back = self.at(self.d), self.at(-self.d)
        self.comm.arrived(self.far_buf, self.device(back), self.sem)
        self.buf[ahead] = (self.buf[ahead].astype(F32) + self.far_buf[...].astype(F32)).astype(BF16)
        self.comm.start(self.buf.at[ahead], self.near_buf.at[0], self.device(ahead), self.sem + 2)

    def total(self):
        own = self.buf[self.i].astype(F32)
        if self.n == 1:
            return own
        ahead, back = self.at(self.d), self.at(-self.d)
        self.comm.arrived(self.near_buf.at[1], self.device(ahead), self.sem + 1)
        self.comm.arrived(self.near_buf.at[0], self.device(back), self.sem + 2)
        return own + self.near_buf[0].astype(F32) + self.near_buf[1].astype(F32)


def kernel(sizes, chunks, block, w_gate, w_up, w_down, out, g_gate, g_up, g_down, *scratch):
    n_zl, n_x, n_zh, n_y, n_c = sizes
    n_dp, n_ex = n_zl * n_x, n_zh * n_y * n_c
    lanes = n_ex * 8
    half = lanes // n_c
    ff, width = w_gate.shape[1], w_gate.shape[2]
    wc = width // chunks
    it = iter(scratch)
    per_chunk = lambda: [next(it) for _ in range(chunks)]
    got, slots, part, x_far, x_near, x_sum, z_near, pair, back, y_far, y_near, y_sum, h_far, h_near = (
        per_chunk() for _ in range(14)
    )
    wgu, wdn, ggu, gdn, picker, unpick, acc_gu, acc_d, act_t = (next(it) for _ in range(9))
    send, recv, local = (next(it) for _ in range(3))

    dp, ex = lax.axis_index("dp"), lax.axis_index("expert")
    x, zl = lax.rem(dp, n_x), lax.div(dp, n_x)
    c, y, zh = lax.rem(ex, n_c), lax.rem(lax.div(ex, n_c), n_y), lax.div(ex, n_c * n_y)

    to_x = lambda v: {"dp": zl * n_x + v, "expert": ex}
    to_zl = lambda v: {"dp": v * n_x + x, "expert": ex}
    to_c = lambda v: {"dp": dp, "expert": (zh * n_y + y) * n_c + v}
    to_y = lambda v: {"dp": dp, "expert": (zh * n_y + v) * n_c + c}
    to_zh = lambda v: {"dp": dp, "expert": (v * n_y + y) * n_c + c}

    loads = [
        pltpu.make_async_copy(w_gate.at[0], wgu.at[pl.ds(0, ff)], local.at[0]),
        pltpu.make_async_copy(w_up.at[0], wgu.at[pl.ds(ff, ff)], local.at[1]),
        pltpu.make_async_copy(w_down.at[0], wdn, local.at[2]),
    ]
    for load in loads:
        load.start()

    partners = []
    for index, size, to in ((x, n_x, to_x), (y, n_y, to_y), (zh, n_zh, to_zh)):
        if size > 1:
            partners += [to(lax.rem(index + 1, size)), to(lax.rem(index + size - 1, size))]
    partners += [to_zl(lax.rem(zl + j, n_zl)) for j in range(1, n_zl)]
    if n_c > 1:
        partners.append(to_c(1 - c))
    barrier = pltpu.get_barrier_semaphore()
    for partner in partners:
        pl.semaphore_signal(barrier, inc=1, device_id=partner, device_id_type=MESH)

    for k in range(chunks):
        lo = 0 if k == 0 else META + k * wc
        got[k][c, y, zh] = block[:, lo : META + (k + 1) * wc]
    pl.semaphore_wait(barrier, len(partners))

    comm = Comm(send, recv)
    in_zh = [RingGather(comm, got[k].at[c, y], zh, n_zh, to_zh, k) for k in range(chunks)]
    in_y = [RingGather(comm, got[k].at[c], y, n_y, to_y, k) for k in range(chunks)]
    in_c = [comm.reserve(1) for k in range(chunks)]
    in_zl = [comm.reserve(3) for k in range(chunks)]
    in_x = [RingGather(comm, slots[k], x, n_x, to_x, k) for k in range(chunks)]
    out_x = [RingReduce(comm, part[k], x_far[k], x_near[k], x, n_x, to_x, k) for k in range(chunks)]
    out_zl = [comm.reserve(3) for k in range(chunks)]
    out_c = [comm.reserve(1) for k in range(chunks)]
    out_y = [RingReduce(comm, back[k], y_far[k], y_near[k], y, n_y, to_y, k) for k in range(chunks)]
    out_zh = [RingReduce(comm, y_sum[k], h_far[k], h_near[k], zh, n_zh, to_zh, k) for k in range(chunks)]

    def make_pickers():
        meta = got[0][:, :, :, :, :META].astype(F32).reshape(lanes, META).astype(BF16)
        eye = ones_where(iota((8, META), 0) == iota((8, META), 1)).astype(BF16)
        facts = nt(eye, meta)
        id0, id1, w0, w1 = (facts[j : j + 1] for j in range(4))
        same = (iota((lanes, lanes), 0) % 8 < 4) == (iota((lanes, lanes), 1) % 8 < 4)
        before = ones_where((iota((lanes, lanes), 0) < iota((lanes, lanes), 1)) & same).astype(BF16)
        slot = iota((2 * SLOTS, lanes), 0)
        is_x = slot < SLOTS
        fits = ones_where(is_x == (iota((2 * SLOTS, lanes), 1) % 8 < 4))
        slot_f = (slot % SLOTS).astype(F32)
        returns = []
        for j in range(n_c):
            expert = (ex if j == 0 else ex + 1 - 2 * c).astype(F32)
            m0, m1 = ones_where(id0 == expert), ones_where(id1 == expert)
            routed = m0 + m1
            weight = m0 * w0 + m1 * w1
            rank = jnp.dot(
                jnp.broadcast_to(routed, (8, lanes)).astype(BF16), before, preferred_element_type=F32
            )[0:1]
            hit = fits * ones_where(slot_f == rank) * routed
            if j == 0:
                picker[...] = jnp.where(is_x, hit, hit * weight).astype(BF16)
            returns.append(jnp.where(is_x, hit * weight, hit))
        flat = jnp.transpose(returns[0] if n_c == 1 else jnp.concatenate(returns, axis=0))
        if n_c == 1:
            unpick[...] = flat.astype(BF16)
        else:
            unpick[...] = jnp.where(c == 0, flat[:half], flat[half:]).astype(BF16)


    def in_core(k):
        in_y[k].finish()
        if n_c > 1:
            comm.start(got[k].at[c], got[k].at[c], to_c(1 - c), in_c[k])

    def in_pick(k):
        if n_c > 1:
            comm.arrived(got[k].at[1 - c], to_c(1 - c), in_c[k])
        if k == 0:
            make_pickers()
        lo = META if k == 0 else 0
        rows = got[k][:, :, :, :, lo:].astype(F32).reshape(lanes, wc).astype(BF16)
        slots[k][x, zl] = jnp.dot(picker[...], rows, preferred_element_type=F32).astype(BF16)
        for j in range(1, n_zl):
            comm.start(slots[k].at[x, zl], slots[k].at[x, zl], to_zl(lax.rem(zl + j, n_zl)), in_zl[k] + j - 1)

    def in_lines(k):
        for j in range(1, n_zl):
            source = lax.rem(zl + n_zl - j, n_zl)
            comm.arrived(slots[k].at[x, source], to_zl(source), in_zl[k] + j - 1)
        in_x[k].near()

    def rows_of(k, at):
        return slots[k][:, :, at : at + SLOTS].reshape(n_dp * SLOTS, wc)

    def in_products(k):
        in_x[k].finish()
        if k == 0:
            for load in loads:
                load.wait()
        cols = slice(k * wc, (k + 1) * wc)
        gu = nt(wgu[:, cols], rows_of(k, 0))
        dn = nt(wdn[:, cols], rows_of(k, SLOTS))
        acc_gu[...] = gu if k == 0 else acc_gu[...] + gu
        acc_d[...] = dn if k == 0 else acc_d[...] + dn

    def in_y_near(k):
        in_zh[k].finish()
        in_y[k].near()

    stages = [
        lambda k: in_zh[k].near(),
        lambda k: in_zh[k].far(),
        in_y_near,
        lambda k: in_y[k].far(),
        in_core,
        in_pick,
        in_lines,
        lambda k: in_x[k].far(),
        in_products,
    ]
    for tick in range(chunks + len(stages) - 1):
        for s in reversed(range(len(stages))):
            if 0 <= tick - s < chunks:
                stages[s](tick - s)


    gate, up, hid_grad = acc_gu[:ff], acc_gu[ff:], acc_d[...]
    sig = jax.nn.sigmoid(gate)
    silu = gate * sig
    hidden = silu * up
    gate_act = hid_grad * up * (sig * (1.0 + gate * (1.0 - sig)))
    up_act = hid_grad * silu
    stacked = jnp.concatenate([hidden, gate_act, up_act], axis=0)
    act_t[0:ff] = hidden.astype(BF16)
    act_t[ff : 2 * ff] = gate_act.astype(BF16)
    act_t[2 * ff : 3 * ff] = up_act.astype(BF16)
    turned = jnp.transpose(stacked).astype(BF16)


    def out_products(k):
        cols = slice(k * wc, (k + 1) * wc)
        shape = (n_x, n_zl, SLOTS, wc)
        o = jnp.dot(turned[:, :ff], wdn[:, cols], preferred_element_type=F32)
        part[k][:, :, 0:SLOTS] = o.astype(BF16).reshape(shape)
        i = jnp.dot(turned[:, ff:], wgu[:, cols], preferred_element_type=F32)
        part[k][:, :, SLOTS:] = i.astype(BF16).reshape(shape)
        out_x[k].first()

    def out_second(k):
        out_x[k].second()
        cols = slice(k * wc, (k + 1) * wc)
        gdn[:, cols] = jnp.dot(act_t[0:ff], rows_of(k, SLOTS), preferred_element_type=F32).astype(BF16)
        ggu[:, cols] = jnp.dot(act_t[ff:], rows_of(k, 0), preferred_element_type=F32).astype(BF16)

    def out_lines(k):
        x_sum[k][...] = out_x[k].total().astype(BF16)
        for j in range(1, n_zl):
            target = lax.rem(zl + j, n_zl)
            comm.start(x_sum[k].at[target], z_near[k].at[j - 1], to_zl(target), out_zl[k] + j - 1)

    def out_core(k):
        total = x_sum[k][zl].astype(F32)
        for j in range(1, n_zl):
            comm.arrived(z_near[k].at[j - 1], to_zl(lax.rem(zl + n_zl - j, n_zl)), out_zl[k] + j - 1)
            total = total + z_near[k][j - 1].astype(F32)
        pair[k][0] = total.astype(BF16)
        if n_c > 1:
            comm.start(pair[k].at[0], pair[k].at[1], to_c(1 - c), out_c[k])

    def out_unpick(k):
        if n_c > 1:
            comm.arrived(pair[k].at[1], to_c(1 - c), out_c[k])
        rows = pair[k][...].reshape(n_c * 2 * SLOTS, wc)
        spread = jnp.dot(unpick[...], rows, preferred_element_type=F32)
        back[k][...] = spread.reshape(n_y, n_zh, 8, wc).astype(BF16)
        out_y[k].first()

    def out_zh_first(k):
        y_sum[k][...] = out_y[k].total().astype(BF16)
        out_zh[k].first()

    def out_store(k):
        out[:, k * wc : (k + 1) * wc] = out_zh[k].total().astype(BF16)

    stages = [
        out_products,
        out_second,
        out_lines,
        out_core,
        out_unpick,
        lambda k: out_y[k].second(),
        out_zh_first,
        lambda k: out_zh[k].second(),
        out_store,
    ]
    stores = []
    for tick in range(chunks + len(stages) - 1):
        for s in reversed(range(len(stages))):
            if 0 <= tick - s < chunks:
                stages[s](tick - s)
        if tick == chunks:
            stores += [
                pltpu.make_async_copy(ggu.at[pl.ds(0, ff)], g_gate.at[0], local.at[3]),
                pltpu.make_async_copy(ggu.at[pl.ds(ff, ff)], g_up.at[0], local.at[4]),
                pltpu.make_async_copy(gdn, g_down.at[0], local.at[5]),
            ]
            for store in stores:
                store.start()
    comm.drain()
    for store in stores:
        store.wait()


def shards(sizes, chunks, tokens, expert_ids, route_weights, out_grad, gate_weight, up_weight, down_weight):
    n_zl, n_x, n_zh, n_y, n_c = sizes
    n_dp, n_ex = n_zl * n_x, n_zh * n_y * n_c
    _, ff, width = gate_weight.shape
    wc = width // chunks
    lanes = n_ex * 8
    facts = jnp.concatenate([expert_ids.astype(BF16), route_weights], axis=1)
    facts = jnp.pad(facts, ((0, 0), (0, META - 4)))
    block = jnp.concatenate(
        [jnp.concatenate([facts, tokens], axis=1), jnp.concatenate([facts, out_grad], axis=1)], axis=0
    )
    vm = lambda *shape: pltpu.VMEM(shape, BF16)
    each = lambda *shape: [vm(*shape) for _ in range(chunks)]
    copies = chunks * 26
    scratch = (
        [vm(n_c, n_y, n_zh, 8, wc + (META if k == 0 else 0)) for k in range(chunks)]
        + each(n_x, n_zl, 2 * SLOTS, wc)
        + each(n_x, n_zl, 2 * SLOTS, wc)
        + each(n_zl, 2 * SLOTS, wc)
        + each(2, n_zl, 2 * SLOTS, wc)
        + each(n_zl, 2 * SLOTS, wc)
        + each(3, 2 * SLOTS, wc)
        + each(n_c, 2 * SLOTS, wc)
        + each(n_y, n_zh, 8, wc)
        + each(n_zh, 8, wc)
        + each(2, n_zh, 8, wc)
        + each(n_zh, 8, wc)
        + each(8, wc)
        + each(2, 8, wc)
        + [
            vm(2 * ff, width), vm(ff, width), vm(2 * ff, width), vm(ff, width),
            vm(2 * SLOTS, lanes), vm(lanes // n_c, n_c * 2 * SLOTS),
            pltpu.VMEM((2 * ff, n_dp * SLOTS), F32), pltpu.VMEM((ff, n_dp * SLOTS), F32),
            vm(3 * ff, n_dp * SLOTS),
            pltpu.SemaphoreType.DMA((copies,)), pltpu.SemaphoreType.DMA((copies,)),
            pltpu.SemaphoreType.DMA((6,)),
        ]
    )
    any_space = pl.BlockSpec(memory_space=pl.ANY)
    vmem = pl.BlockSpec(memory_space=pltpu.VMEM)
    rows, g_gate, g_up, g_down = pl.pallas_call(
        functools.partial(kernel, sizes, chunks),
        out_shape=(
            jax.ShapeDtypeStruct((8, width), BF16),
            jax.ShapeDtypeStruct(gate_weight.shape, BF16),
            jax.ShapeDtypeStruct(gate_weight.shape, BF16),
            jax.ShapeDtypeStruct(gate_weight.shape, BF16),
        ),
        in_specs=[vmem, any_space, any_space, any_space],
        out_specs=(vmem, any_space, any_space, any_space),
        scratch_shapes=scratch,
        compiler_params=pltpu.CompilerParams(
            collective_id=0, has_side_effects=True, vmem_limit_bytes=56 * 2**20
        ),
        name="experts",
    )(block, gate_weight, up_weight, down_weight)
    return rows[:4], rows[4:], g_gate, g_up, g_down


def solution(mesh):
    rows, held = P(("dp", "expert"), None), P("expert", "dp", None)
    return jax.shard_map(
        functools.partial(shards, SIZES, CHUNKS),
        mesh=mesh,
        in_specs=(rows, rows, rows, rows, held, held, held),
        out_specs=(rows, rows, held, held, held),
        check_vma=False,
    )
```

time: 614 us -> 165 us (0.27)
  the two profiles are of different devices: /device:TPU:1 before, /device:TPU:2 now
where the time goes in v1:
time: 165 us; the launch traced here: 164 us
  Pallas kernels  155 us (94%)
  local copies, waits for them, and re-layouts  6.77 us (4%)
  other arithmetic  2.2 us (1%)
    pallas_call x1, Pallas kernels, shards(): pl.pallas_call(functools.partial(kernel, sizes, chunks), out_shape=(jax.S...  155 us
    unnamed x10, local copies, waits for them, and re-layouts  5.09 us

profile of v1, /device:TPU:2, one launch (start us, length us, event | category | flops | bytes accessed | tf_op | source)
XLA Modules:
  0.0 164.3 jit_solution(3412213298998261340)
XLA Ops:
  0.6 0.7 convert_element_type.5
  1.3 0.0 copy-start.2
  1.3 0.1 copy.14
  1.4 0.5 copy-done.2
  2.0 0.1 copy.15
  2.1 0.1 fusion.2
  2.2 1.4 maximum_maximum_fusion.block
  3.6 154.7 %experts.1 = (bf16[8,4096]{1,0:T(8,128)(2,1)}, bf16[1,96,4096]{2,1,0:T(8,128)(2,1)}, bf16[1,96,4096]{2,1,0:T(8,128)(2,1)}, bf16[1,96,4096]{2,1,0:T(8,128)(2,1)}) custom-call(bf16[8,4224]{1,0:T(8,128)(2,1)} %maximum_maximum_fusion.block, bf16[1,96,4096]{2,1,0:T(8,128)(2,1)} %w_gate.1, bf16[1,96,4096]{2,1,0:T(8,128)(2,1)} %w_up.1, bf16[1,96,4096]{2,1,0:T(8,128)(2,1)} %w_down.1), custom_call_target="tpu_custom_call" | custom-call | tf_op jit(solution)/shard_map/experts/pallas_call | solution.py:400
  158.3 1.6 fusion.3
  159.9 0.0 copy-start.1
  159.9 2.1 %copy.19 = bf16[1,96,4096]{2,1,0:T(8,128)(2,1)} copy(bf16[1,96,4096]{2,1,0:T(8,128)(2,1)} %get-tuple-element.22) | data formatting | bytes 1572864
  162.0 0.0 copy-done.1
  162.0 0.0 copy-start
  162.0 0.9 copy.20
  162.9 0.5 copy-done
  163.4 0.9 copy.21
Async XLA Ops:
  1.3 0.7 copy-start.2
  159.9 2.1 %copy-start.1 = (bf16[1,96,4096]{2,1,0:T(8,128)(2,1)S(1)}, bf16[1,96,4096]{2,1,0:T(8,128)(2,1)}, u32[]{:S(2)}) copy-start(bf16[1,96,4096]{2,1,0:T(8,128)(2,1)} %get-tuple-element.23) | copy-start | bytes 2359300
  162.0 1.4 copy-start

commit v2 on v1

v2 whole, which is shorter than its diff:
```python
import functools

import jax
import jax.numpy as jnp
from jax import lax
from jax.experimental import pallas as pl
from jax.experimental.pallas import tpu as pltpu
from jax.sharding import PartitionSpec as P

SIZES = (4, 4, 4, 4, 2)
PIECES = 4
ORDER = (
    0, 1, 2, 10, 3, 11, 4, 12, 5, 20, 13, 6, 21, 14, 7, 22, 15, 30, 23, 16, 24, 40, 31, 17, 25, 41, 32, 26, 42, 33, 43,
    34, 50, 27, 44, 35, 51, 45, 36, 60, 46, 52, 37, 61, 47, 53, 70, 54, 62, 71, 55, 63, 56, 64, 57, 72, 65, 73, 81, 90,
    91, 66, 74, 67, 75, 100, 92, 101, 93, 76, 77, 82, 110, 120, 111, 112, 121, 102, 94, 113, 130, 103, 95, 140, 122, 131,
    114, 115, 141, 104, 96, 123, 150, 116, 132, 117, 151, 142, 105, 124, 97, 133, 160, 143, 161, 152, 106, 125, 134, 170,
    107, 144, 162, 153, 171, 126, 135, 127, 163, 145, 154, 172, 136, 146, 155, 137, 173, 164, 147, 165, 156, 174, 157,
    175, 166, 167, 176, 177,
)
SLOTS = 16
META = 128
F32 = jnp.float32
BF16 = jnp.bfloat16
MESH = pl.DeviceIdType.MESH


def nt(left, right):
    return lax.dot_general(left, right, (((1,), (1,)), ((), ())), preferred_element_type=F32)


def iota(shape, dim):
    return lax.broadcasted_iota(jnp.int32, shape, dim)


def ones_where(mask):
    return jnp.where(mask, 1.0, 0.0).astype(F32)


class Comm:
    def __init__(self, send, recv):
        self.send, self.recv, self.count, self.sent = send, recv, 0, []

    def reserve(self, amount):
        at = self.count
        self.count += amount
        return at

    def start(self, src, dst, device, sem):
        copy = pltpu.make_async_remote_copy(
            src_ref=src, dst_ref=dst, send_sem=self.send.at[sem], recv_sem=self.recv.at[sem],
            device_id=device, device_id_type=MESH,
        )
        copy.start()
        self.sent.append(copy)

    def arrived(self, dst, device, sem):
        pltpu.make_async_remote_copy(
            src_ref=dst, dst_ref=dst, send_sem=self.send.at[sem], recv_sem=self.recv.at[sem],
            device_id=device, device_id_type=MESH,
        ).wait_recv()

    def drain(self):
        for copy in self.sent:
            copy.wait_send()


class RingGather:
    def __init__(self, comm, buf, index, size, device, turn):
        self.comm, self.buf, self.i, self.n, self.device = comm, buf, index, size, device
        self.d = 1 if turn % 2 == 0 else -1
        self.sem = comm.reserve(3) if size > 1 else 0

    def at(self, step):
        return lax.rem(self.i + step + self.n, self.n)

    def near(self):
        if self.n == 1:
            return
        for j, step in enumerate((self.d, -self.d)):
            self.comm.start(self.buf.at[self.i], self.buf.at[self.i], self.device(self.at(step)), self.sem + j)

    def far(self):
        if self.n == 1:
            return
        back, ahead = self.at(-self.d), self.at(self.d)
        self.comm.arrived(self.buf.at[back], self.device(back), self.sem)
        self.comm.start(self.buf.at[back], self.buf.at[back], self.device(ahead), self.sem + 2)

    def finish(self):
        if self.n == 1:
            return
        ahead = self.at(self.d)
        self.comm.arrived(self.buf.at[ahead], self.device(ahead), self.sem + 1)
        self.comm.arrived(self.buf.at[self.at(2)], self.device(self.at(-self.d)), self.sem + 2)


class Spread:
    def __init__(self, comm, buf, index, size, device):
        self.comm, self.buf, self.i, self.n, self.device = comm, buf, index, size, device
        self.sem = comm.reserve(size - 1)

    def send(self):
        for j in range(1, self.n):
            self.comm.start(
                self.buf.at[self.i], self.buf.at[self.i], self.device(lax.rem(self.i + j, self.n)), self.sem + j - 1
            )

    def finish(self):
        for j in range(1, self.n):
            source = lax.rem(self.i + self.n - j, self.n)
            self.comm.arrived(self.buf.at[source], self.device(source), self.sem + j - 1)


class Collect:
    def __init__(self, comm, buf, near_buf, index, size, device):
        self.comm, self.buf, self.near_buf, self.i, self.n, self.device = comm, buf, near_buf, index, size, device
        self.sem = comm.reserve(size - 1)

    def send(self):
        for j in range(1, self.n):
            target = lax.rem(self.i + j, self.n)
            self.comm.start(self.buf.at[target], self.near_buf.at[j - 1], self.device(target), self.sem + j - 1)

    def total(self):
        value = self.buf[self.i].astype(F32)
        for j in range(1, self.n):
            source = lax.rem(self.i + self.n - j, self.n)
            self.comm.arrived(self.near_buf.at[j - 1], self.device(source), self.sem + j - 1)
            value = value + self.near_buf[j - 1].astype(F32)
        return value


class RingReduce:
    def __init__(self, comm, buf, far_buf, near_buf, index, size, device, turn):
        self.comm, self.buf, self.far_buf, self.near_buf = comm, buf, far_buf, near_buf
        self.i, self.n, self.device = index, size, device
        self.d = 1 if turn % 2 == 0 else -1
        self.sem = comm.reserve(3) if size > 1 else 0

    def at(self, step):
        return lax.rem(self.i + step + self.n, self.n)

    def first(self):
        if self.n == 1:
            return
        ahead, back = self.at(self.d), self.at(-self.d)
        self.comm.start(self.buf.at[self.at(2)], self.far_buf, self.device(ahead), self.sem)
        self.comm.start(self.buf.at[back], self.near_buf.at[1], self.device(back), self.sem + 1)

    def second(self):
        if self.n == 1:
            return
        ahead, back = self.at(self.d), self.at(-self.d)
        self.comm.arrived(self.far_buf, self.device(back), self.sem)
        self.buf[ahead] = (self.buf[ahead].astype(F32) + self.far_buf[...].astype(F32)).astype(BF16)
        self.comm.start(self.buf.at[ahead], self.near_buf.at[0], self.device(ahead), self.sem + 2)

    def total(self):
        own = self.buf[self.i].astype(F32)
        if self.n == 1:
            return own
        ahead, back = self.at(self.d), self.at(-self.d)
        self.comm.arrived(self.near_buf.at[1], self.device(ahead), self.sem + 1)
        self.comm.arrived(self.near_buf.at[0], self.device(back), self.sem + 2)
        return own + self.near_buf[0].astype(F32) + self.near_buf[1].astype(F32)


def kernel(
    sizes, pieces, tokens, out_grad, meta, w_gate, w_up, w_down, mixed, in_grad, g_gate, g_up, g_down, *scratch
):
    n_zl, n_x, n_zh, n_y, n_c = sizes
    n_dp, n_ex = n_zl * n_x, n_zh * n_y * n_c
    lanes = n_ex * 8
    half = lanes // n_c
    ff, width = w_gate.shape[1], w_gate.shape[2]
    wc = width // pieces
    hw = wc // 2
    items = range(2 * pieces)
    it = iter(scratch)
    per_item = lambda: [next(it) for _ in items]
    got, slots, part, x_far, x_near, x_sum, z_near, pair, back, y_near, y_sum, h_far, h_near = (
        per_item() for _ in range(13)
    )
    wgu, wdn, ggu, gdn, pick_x, pick_g, back_o, back_i, acc_gu, acc_d, hid, hid_t, gu, gu_t = (
        next(it) for _ in range(14)
    )
    send, recv, local = (next(it) for _ in range(3))

    dp, ex = lax.axis_index("dp"), lax.axis_index("expert")
    x, zl = lax.rem(dp, n_x), lax.div(dp, n_x)
    c, y, zh = lax.rem(ex, n_c), lax.rem(lax.div(ex, n_c), n_y), lax.div(ex, n_c * n_y)

    to_x = lambda v: {"dp": zl * n_x + v, "expert": ex}
    to_zl = lambda v: {"dp": v * n_x + x, "expert": ex}
    to_c = lambda v: {"dp": dp, "expert": (zh * n_y + y) * n_c + v}
    to_y = lambda v: {"dp": dp, "expert": (zh * n_y + v) * n_c + c}
    to_zh = lambda v: {"dp": dp, "expert": (v * n_y + y) * n_c + c}

    partners = []
    for index, size, to in ((x, n_x, to_x), (zh, n_zh, to_zh)):
        if size > 1:
            partners += [to(lax.rem(index + 1, size)), to(lax.rem(index + size - 1, size))]
    partners += [to_zl(lax.rem(zl + j, n_zl)) for j in range(1, n_zl)]
    partners += [to_y(lax.rem(y + j, n_y)) for j in range(1, n_y)]
    if n_c > 1:
        partners.append(to_c(1 - c))
    barrier = pltpu.get_barrier_semaphore()
    for partner in partners:
        pl.semaphore_signal(barrier, inc=1, device_id=partner, device_id_type=MESH)

    loads = [
        pltpu.make_async_copy(w_gate.at[0], wgu.at[pl.ds(0, ff)], local.at[0]),
        pltpu.make_async_copy(w_up.at[0], wgu.at[pl.ds(ff, ff)], local.at[1]),
        pltpu.make_async_copy(w_down.at[0], wdn, local.at[2]),
    ]
    for load in loads:
        load.start()

    def piece(k):
        lo = k % pieces * wc
        return slice(lo, lo + wc)

    for k in items:
        source, lo = tokens if k < pieces else out_grad, k % pieces * wc
        own = jnp.concatenate(
            [source[:, lo : lo + hw].astype(F32), source[:, lo + hw : lo + wc].astype(F32)], axis=0
        ).astype(BF16)
        if k == 0:
            got[k][c, y, zh, :, :META] = meta[...]
            got[k][c, y, zh, :, META:] = own
        else:
            got[k][c, y, zh] = own
    pl.semaphore_wait(barrier, len(partners))

    comm = Comm(send, recv)
    in_zh = [RingGather(comm, got[k].at[c, y], zh, n_zh, to_zh, k) for k in items]
    in_y = [Spread(comm, got[k].at[c], y, n_y, to_y) for k in items]
    in_c = [comm.reserve(1) for k in items]
    in_zl = [Spread(comm, slots[k].at[x], zl, n_zl, to_zl) for k in items]
    in_x = [RingGather(comm, slots[k], x, n_x, to_x, k) for k in items]
    out_x = [RingReduce(comm, part[k], x_far[k], x_near[k], x, n_x, to_x, k) for k in items]
    out_zl = [Collect(comm, x_sum[k], z_near[k], zl, n_zl, to_zl) for k in items]
    out_c = [comm.reserve(1) for k in items]
    out_y = [Collect(comm, back[k], y_near[k], y, n_y, to_y) for k in items]
    out_zh = [RingReduce(comm, y_sum[k], h_far[k], h_near[k], zh, n_zh, to_zh, k) for k in items]

    def make_pickers():
        rows = got[0][:, :, :, :, :META].astype(F32).reshape(lanes, META).astype(BF16)
        eye = ones_where(iota((8, META), 0) == iota((8, META), 1)).astype(BF16)
        facts = nt(eye, rows)
        id0, id1, w0, w1 = (facts[j : j + 1] for j in range(4))
        same = (iota((lanes, lanes), 0) % 8 < 4) == (iota((lanes, lanes), 1) % 8 < 4)
        before = ones_where((iota((lanes, lanes), 0) < iota((lanes, lanes), 1)) & same).astype(BF16)
        slot = iota((2 * SLOTS, lanes), 0)
        fits = ones_where((slot < SLOTS) == (iota((2 * SLOTS, lanes), 1) % 8 < 4))
        slot_f = (slot % SLOTS).astype(F32)
        plain, weighted = [], []
        for j in range(n_c):
            expert = (ex if j == 0 else ex + 1 - 2 * c).astype(F32)
            m0, m1 = ones_where(id0 == expert), ones_where(id1 == expert)
            routed = m0 + m1
            rank = jnp.dot(
                jnp.broadcast_to(routed, (8, lanes)).astype(BF16), before, preferred_element_type=F32
            )[0:1]
            hit = fits * ones_where(slot_f == rank) * routed
            plain.append(hit)
            weighted.append(hit * (m0 * w0 + m1 * w1))
        pick_x[...] = plain[0].astype(BF16)
        pick_g[...] = weighted[0].astype(BF16)
        for ref, parts in ((back_i, plain), (back_o, weighted)):
            flat = jnp.transpose(parts[0] if n_c == 1 else jnp.concatenate(parts, axis=0))
            ref[...] = (flat if n_c == 1 else jnp.where(c == 0, flat[:half], flat[half:])).astype(BF16)


    def in_y_send(k):
        in_zh[k].finish()
        in_y[k].send()

    def in_core(k):
        in_y[k].finish()
        if n_c > 1:
            comm.start(got[k].at[c], got[k].at[c], to_c(1 - c), in_c[k])

    def in_pick(k):
        if n_c > 1:
            comm.arrived(got[k].at[1 - c], to_c(1 - c), in_c[k])
        if k == 0:
            make_pickers()
        lo = META if k == 0 else 0
        rows = got[k][:, :, :, :, lo:].astype(F32).reshape(lanes, hw).astype(BF16)
        picker = pick_x if k < pieces else pick_g
        picked = jnp.dot(picker[...], rows, preferred_element_type=F32).astype(BF16)
        slots[k][x, zl, :, :hw] = picked[:SLOTS]
        slots[k][x, zl, :, hw:] = picked[SLOTS:]
        in_zl[k].send()

    def in_x_near(k):
        in_zl[k].finish()
        in_x[k].near()

    def rows_of(k):
        return slots[k][...].reshape(n_dp * SLOTS, wc)

    def in_products(k):
        in_x[k].finish()
        if k == 0:
            for load in loads:
                load.wait()
        weights, total = (wgu, acc_gu) if k < pieces else (wdn, acc_d)
        product = nt(weights[:, piece(k)], rows_of(k))
        total[...] = product if k % pieces == 0 else total[...] + product


    def activate(k):
        if k == 1:
            gate, up = acc_gu[:ff], acc_gu[ff:]
            sig = jax.nn.sigmoid(gate)
            silu = gate * sig
            hidden = silu * up
            hid[...] = hidden.astype(BF16)
            hid_t[...] = jnp.transpose(hidden).astype(BF16)
            acc_gu[:ff] = up * (sig * (1.0 + gate * (1.0 - sig)))
            acc_gu[ff:] = silu
        else:
            grad = acc_d[...]
            both = jnp.concatenate([grad * acc_gu[:ff], grad * acc_gu[ff:]], axis=0)
            gu[...] = both.astype(BF16)
            gu_t[...] = jnp.transpose(both).astype(BF16)


    def out_products(k):
        left, weights = (hid_t, wdn) if k < pieces else (gu_t, wgu)
        product = jnp.dot(left[...], weights[:, piece(k)], preferred_element_type=F32)
        part[k][...] = product.astype(BF16).reshape(n_x, n_zl, SLOTS, wc)
        out_x[k].first()

    stores = []

    def weight_grads(k):
        left, held = (gu, ggu) if k < pieces else (hid, gdn)
        held[:, piece(k)] = jnp.dot(left[...], rows_of(k), preferred_element_type=F32).astype(BF16)
        pairs = ((ggu, 0, g_gate), (ggu, ff, g_up)) if k < pieces else ((gdn, 0, g_down),)
        for ref, at, target in pairs:
            store = pltpu.make_async_copy(
                ref.at[pl.ds(at, ff), piece(k)], target.at[0, :, piece(k)], local.at[3 + len(stores)]
            )
            store.start()
            stores.append(store)

    def out_lines(k):
        x_sum[k][...] = out_x[k].total().astype(BF16)
        out_zl[k].send()

    def out_core(k):
        total = out_zl[k].total().astype(BF16)
        pair[k][0, :SLOTS] = total[:, :hw]
        pair[k][0, SLOTS:] = total[:, hw:]
        if n_c > 1:
            comm.start(pair[k].at[0], pair[k].at[1], to_c(1 - c), out_c[k])

    def out_back(k):
        if n_c > 1:
            comm.arrived(pair[k].at[1], to_c(1 - c), out_c[k])
        rows = pair[k][...].reshape(n_c * 2 * SLOTS, hw)
        spread = jnp.dot((back_o if k < pieces else back_i)[...], rows, preferred_element_type=F32)
        back[k][...] = spread.reshape(n_y, n_zh, 8, hw).astype(BF16)
        out_y[k].send()

    def out_zh_first(k):
        y_sum[k][...] = out_y[k].total().astype(BF16)
        out_zh[k].first()

    def out_store(k):
        total = out_zh[k].total()
        target, lo = mixed if k < pieces else in_grad, k % pieces * wc
        target[:, lo : lo + hw] = total[:4].astype(BF16)
        target[:, lo + hw : lo + wc] = total[4:].astype(BF16)

    steps = (
        lambda k: in_zh[k].near(),
        lambda k: in_zh[k].far(),
        in_y_send,
        in_core,
        in_pick,
        in_x_near,
        lambda k: in_x[k].far(),
        in_products,
        activate,
        out_products,
        lambda k: out_x[k].second(),
        weight_grads,
        out_lines,
        out_core,
        out_back,
        out_zh_first,
        lambda k: out_zh[k].second(),
        out_store,
    )
    for entry in ORDER:
        steps[entry // 10](entry % 10)
    comm.drain()
    for store in stores:
        store.wait()


def shards(sizes, pieces, tokens, expert_ids, route_weights, out_grad, gate_weight, up_weight, down_weight):
    n_zl, n_x, n_zh, n_y, n_c = sizes
    n_dp, n_ex = n_zl * n_x, n_zh * n_y * n_c
    _, ff, width = gate_weight.shape
    wc = width // pieces
    hw = wc // 2
    lanes = n_ex * 8
    facts = jnp.concatenate([expert_ids.astype(BF16), route_weights], axis=1)
    meta = jnp.pad(jnp.concatenate([facts, facts], axis=0), ((0, 0), (0, META - 4)))
    vm = lambda *shape: pltpu.VMEM(shape, BF16)
    fl = lambda *shape: pltpu.VMEM(shape, F32)
    each = lambda *shape: [vm(*shape) for _ in range(2 * pieces)]
    copies = 2 * pieces * 26
    scratch = (
        [vm(n_c, n_y, n_zh, 8, hw + (META if k == 0 else 0)) for k in range(2 * pieces)]
        + each(n_x, n_zl, SLOTS, wc)
        + each(n_x, n_zl, SLOTS, wc)
        + each(n_zl, SLOTS, wc)
        + each(2, n_zl, SLOTS, wc)
        + each(n_zl, SLOTS, wc)
        + each(3, SLOTS, wc)
        + each(n_c, 2 * SLOTS, hw)
        + each(n_y, n_zh, 8, hw)
        + each(3, n_zh, 8, hw)
        + each(n_zh, 8, hw)
        + each(8, hw)
        + each(2, 8, hw)
        + [
            vm(2 * ff, width), vm(ff, width), vm(2 * ff, width), vm(ff, width),
            vm(2 * SLOTS, lanes), vm(2 * SLOTS, lanes),
            vm(lanes // n_c, n_c * 2 * SLOTS), vm(lanes // n_c, n_c * 2 * SLOTS),
            fl(2 * ff, n_dp * SLOTS), fl(ff, n_dp * SLOTS),
            vm(ff, n_dp * SLOTS), vm(n_dp * SLOTS, ff), vm(2 * ff, n_dp * SLOTS), vm(n_dp * SLOTS, 2 * ff),
            pltpu.SemaphoreType.DMA((copies,)), pltpu.SemaphoreType.DMA((copies,)),
            pltpu.SemaphoreType.DMA((3 + 3 * pieces,)),
        ]
    )
    any_space = pl.BlockSpec(memory_space=pl.ANY)
    vmem = pl.BlockSpec(memory_space=pltpu.VMEM)
    like = lambda a: jax.ShapeDtypeStruct(a.shape, BF16)
    return pl.pallas_call(
        functools.partial(kernel, sizes, pieces),
        out_shape=(like(tokens), like(tokens), like(gate_weight), like(gate_weight), like(gate_weight)),
        in_specs=[vmem, vmem, vmem, any_space, any_space, any_space],
        out_specs=(vmem, vmem, any_space, any_space, any_space),
        scratch_shapes=scratch,
        compiler_params=pltpu.CompilerParams(
            collective_id=0, has_side_effects=True, vmem_limit_bytes=56 * 2**20
        ),
        name="experts",
    )(tokens, out_grad, meta, gate_weight, up_weight, down_weight)


def solution(mesh):
    rows, held = P(("dp", "expert"), None), P("expert", "dp", None)
    return jax.shard_map(
        functools.partial(shards, SIZES, PIECES),
        mesh=mesh,
        in_specs=(rows, rows, rows, rows, held, held, held),
        out_specs=(rows, rows, held, held, held),
        check_vma=False,
    )
```

time: 165 us -> 147 us (0.89)
  the two profiles are of different devices: /device:TPU:2 before, /device:TPU:1 now
where the time goes in v2:
time: 147 us; the launch traced here: 145 us
  Pallas kernels  135 us (92%)
  local copies, waits for them, and re-layouts  7.2 us (5%)
    pallas_call x1, Pallas kernels, shards(): pl.pallas_call(functools.partial(kernel, sizes, pieces), out_shape=(like(...  135 us
    unnamed x14, local copies, waits for them, and re-layouts  7.1 us

profile of v2, /device:TPU:1, one launch (start us, length us, event | category | flops | bytes accessed | tf_op | source)
XLA Modules:
  0.0 144.6 jit_solution(6571311262039805356)
XLA Ops:
  0.6 0.7 convert_element_type.5
  1.3 0.0 copy-start.3
  1.3 0.1 copy.14
  1.4 0.5 copy-done.3
  2.0 0.1 copy.15
  2.1 0.7 fusion.5.meta
  2.7 135.4 %experts.1 = (bf16[4,4096]{1,0:T(4,128)(2,1)}, bf16[4,4096]{1,0:T(4,128)(2,1)}, bf16[1,96,4096]{2,1,0:T(8,128)(2,1)}, bf16[1,96,4096]{2,1,0:T(8,128)(2,1)}, bf16[1,96,4096]{2,1,0:T(8,128)(2,1)}) custom-call(bf16[4,4096]{1,0:T(4,128)(2,1)} %tokens.1, bf16[4,4096]{1,0:T(4,128)(2,1)} %out_grad.1, bf16[8,128]{1,0:T(8,128)(2,1)} %fusion.5.meta, ...), custom_call_target="tpu_custom_call" | custom-call | tf_op jit(solution)/shard_map/experts/pallas_call | solution.py:446
  138.1 0.0 copy-start.2
  138.1 1.4 copy.21
  139.5 0.0 copy-done.2
  139.5 0.6 copy.22
  140.1 0.0 copy-start.1
  140.1 2.1 %copy.23 = bf16[1,96,4096]{2,1,0:T(8,128)(2,1)} copy(bf16[1,96,4096]{2,1,0:T(8,128)(2,1)} %get-tuple-element.12) | data formatting | bytes 1572864
  142.3 0.0 copy-done.1
  142.3 0.0 copy-start
  142.3 0.9 copy.24
  143.1 0.5 copy-done
  143.7 0.9 copy.25
Async XLA Ops:
  1.3 0.7 copy-start.3
  138.1 1.4 copy-start.2
  140.1 2.1 %copy-start.1 = (bf16[1,96,4096]{2,1,0:T(8,128)(2,1)S(1)}, bf16[1,96,4096]{2,1,0:T(8,128)(2,1)}, u32[]{:S(2)}) copy-start(bf16[1,96,4096]{2,1,0:T(8,128)(2,1)} %get-tuple-element.13) | copy-start | bytes 2359300
  142.3 1.4 copy-start

commit v3 on v2

--- a/solution.py
+++ b/solution.py
@@ -10,12 +10,11 @@
 SIZES = (4, 4, 4, 4, 2)
 PIECES = 4
 ORDER = (
-    0, 1, 2, 10, 3, 11, 4, 12, 5, 20, 13, 6, 21, 14, 7, 22, 15, 30, 23, 16, 24, 40, 31, 17, 25, 41, 32, 26, 42, 33, 43,
-    34, 50, 27, 44, 35, 51, 45, 36, 60, 46, 52, 37, 61, 47, 53, 70, 54, 62, 71, 55, 63, 56, 64, 57, 72, 65, 73, 81, 90,
-    91, 66, 74, 67, 75, 100, 92, 101, 93, 76, 77, 82, 110, 120, 111, 112, 121, 102, 94, 113, 130, 103, 95, 140, 122, 131,
-    114, 115, 141, 104, 96, 123, 150, 116, 132, 117, 151, 142, 105, 124, 97, 133, 160, 143, 161, 152, 106, 125, 134, 170,
-    107, 144, 162, 153, 171, 126, 135, 127, 163, 145, 154, 172, 136, 146, 155, 137, 173, 164, 147, 165, 156, 174, 157,
-    175, 166, 167, 176, 177,
+    0, 1, 2, 3, 4, 5, 6, 7, 10, 11, 12, 13, 20, 14, 30, 21, 15, 22, 16, 31, 32, 23, 17, 24, 25, 40, 33, 26, 27, 41,
+    34, 42, 35, 50, 43, 36, 51, 44, 37, 52, 45, 60, 53, 61, 46, 54, 47, 62, 55, 63, 71, 80, 81, 56, 64, 57, 65, 90,
+    82, 91, 83, 66, 67, 72, 100, 101, 102, 103, 110, 104, 105, 106, 107, 92, 111, 84, 93, 85, 120, 130, 112, 121,
+    94, 131, 86, 113, 140, 95, 87, 122, 141, 114, 132, 123, 96, 115, 133, 142, 97, 150, 151, 124, 116, 134, 143,
+    125, 135, 117, 144, 152, 126, 136, 145, 153, 127, 137, 146, 154, 155, 147, 156, 157,
 )
 SLOTS = 16
 META = 128
@@ -178,11 +177,11 @@
     items = range(2 * pieces)
     it = iter(scratch)
     per_item = lambda: [next(it) for _ in items]
-    got, slots, part, x_far, x_near, x_sum, z_near, pair, back, y_near, y_sum, h_far, h_near = (
-        per_item() for _ in range(13)
+    got, slots, part, x_far, x_near, x_sum, z_near, pair, back, y_near, y_sum, h_near = (
+        per_item() for _ in range(12)
     )
-    wgu, wdn, ggu, gdn, pick_x, pick_g, back_o, back_i, acc_gu, acc_d, hid, hid_t, gu, gu_t = (
-        next(it) for _ in range(14)
+    wgu, wdn, ggu, gdn, pick_x, pick_g, back_o, back_i, acc_gu, acc_d, hid, hid_t, gu, gu_t, before, plain, weighted = (
+        next(it) for _ in range(17)
     )
     send, recv, local = (next(it) for _ in range(3))
 
@@ -197,11 +196,10 @@
     to_zh = lambda v: {"dp": dp, "expert": (v * n_y + y) * n_c + c}
 
     partners = []
-    for index, size, to in ((x, n_x, to_x), (zh, n_zh, to_zh)):
-        if size > 1:
-            partners += [to(lax.rem(index + 1, size)), to(lax.rem(index + size - 1, size))]
-    partners += [to_zl(lax.rem(zl + j, n_zl)) for j in range(1, n_zl)]
-    partners += [to_y(lax.rem(y + j, n_y)) for j in range(1, n_y)]
+    for index, size, to in ((zh, n_zh, to_zh), (y, n_y, to_y), (zl, n_zl, to_zl)):
+        partners += [to(lax.rem(index + j, size)) for j in range(1, size)]
+    if n_x > 1:
+        partners += [to_x(lax.rem(x + 1, n_x)), to_x(lax.rem(x + n_x - 1, n_x))]
     if n_c > 1:
         partners.append(to_c(1 - c))
     barrier = pltpu.get_barrier_semaphore()
@@ -230,10 +228,12 @@
             got[k][c, y, zh, :, META:] = own
         else:
             got[k][c, y, zh] = own
+    same = (iota((lanes, lanes), 0) % 8 < 4) == (iota((lanes, lanes), 1) % 8 < 4)
+    before[...] = ones_where((iota((lanes, lanes), 0) < iota((lanes, lanes), 1)) & same).astype(BF16)
     pl.semaphore_wait(barrier, len(partners))
 
     comm = Comm(send, recv)
-    in_zh = [RingGather(comm, got[k].at[c, y], zh, n_zh, to_zh, k) for k in items]
+    in_zh = [Spread(comm, got[k].at[c, y], zh, n_zh, to_zh) for k in items]
     in_y = [Spread(comm, got[k].at[c], y, n_y, to_y) for k in items]
     in_c = [comm.reserve(1) for k in items]
     in_zl = [Spread(comm, slots[k].at[x], zl, n_zl, to_zl) for k in items]
@@ -242,33 +242,32 @@
     out_zl = [Collect(comm, x_sum[k], z_near[k], zl, n_zl, to_zl) for k in items]
     out_c = [comm.reserve(1) for k in items]
     out_y = [Collect(comm, back[k], y_near[k], y, n_y, to_y) for k in items]
-    out_zh = [RingReduce(comm, y_sum[k], h_far[k], h_near[k], zh, n_zh, to_zh, k) for k in items]
+    out_zh = [Collect(comm, y_sum[k], h_near[k], zh, n_zh, to_zh) for k in items]
 
     def make_pickers():
         rows = got[0][:, :, :, :, :META].astype(F32).reshape(lanes, META).astype(BF16)
         eye = ones_where(iota((8, META), 0) == iota((8, META), 1)).astype(BF16)
         facts = nt(eye, rows)
         id0, id1, w0, w1 = (facts[j : j + 1] for j in range(4))
-        same = (iota((lanes, lanes), 0) % 8 < 4) == (iota((lanes, lanes), 1) % 8 < 4)
-        before = ones_where((iota((lanes, lanes), 0) < iota((lanes, lanes), 1)) & same).astype(BF16)
         slot = iota((2 * SLOTS, lanes), 0)
         fits = ones_where((slot < SLOTS) == (iota((2 * SLOTS, lanes), 1) % 8 < 4))
         slot_f = (slot % SLOTS).astype(F32)
-        plain, weighted = [], []
         for j in range(n_c):
             expert = (ex if j == 0 else ex + 1 - 2 * c).astype(F32)
             m0, m1 = ones_where(id0 == expert), ones_where(id1 == expert)
             routed = m0 + m1
             rank = jnp.dot(
-                jnp.broadcast_to(routed, (8, lanes)).astype(BF16), before, preferred_element_type=F32
+                jnp.broadcast_to(routed, (8, lanes)).astype(BF16), before[...], preferred_element_type=F32
             )[0:1]
             hit = fits * ones_where(slot_f == rank) * routed
-            plain.append(hit)
-            weighted.append(hit * (m0 * w0 + m1 * w1))
-        pick_x[...] = plain[0].astype(BF16)
-        pick_g[...] = weighted[0].astype(BF16)
-        for ref, parts in ((back_i, plain), (back_o, weighted)):
-            flat = jnp.transpose(parts[0] if n_c == 1 else jnp.concatenate(parts, axis=0))
+            plain[2 * SLOTS * j : 2 * SLOTS * (j + 1)] = hit
+            weighted[2 * SLOTS * j : 2 * SLOTS * (j + 1)] = hit * (m0 * w0 + m1 * w1)
+        pick_x[...] = plain[: 2 * SLOTS].astype(BF16)
+        pick_g[...] = weighted[: 2 * SLOTS].astype(BF16)
+
+    def turn_pickers():
+        for ref, held in ((back_i, plain), (back_o, weighted)):
+            flat = jnp.transpose(held[...])
             ref[...] = (flat if n_c == 1 else jnp.where(c == 0, flat[:half], flat[half:])).astype(BF16)
 
 
@@ -293,6 +292,8 @@
         slots[k][x, zl, :, :hw] = picked[:SLOTS]
         slots[k][x, zl, :, hw:] = picked[SLOTS:]
         in_zl[k].send()
+        if k == 0:
+            turn_pickers()
 
     def in_x_near(k):
         in_zl[k].finish()
@@ -366,9 +367,9 @@
         back[k][...] = spread.reshape(n_y, n_zh, 8, hw).astype(BF16)
         out_y[k].send()
 
-    def out_zh_first(k):
+    def out_zh_send(k):
         y_sum[k][...] = out_y[k].total().astype(BF16)
-        out_zh[k].first()
+        out_zh[k].send()
 
     def out_store(k):
         total = out_zh[k].total()
@@ -377,8 +378,7 @@
         target[:, lo + hw : lo + wc] = total[4:].astype(BF16)
 
     steps = (
-        lambda k: in_zh[k].near(),
-        lambda k: in_zh[k].far(),
+        lambda k: in_zh[k].send(),
         in_y_send,
         in_core,
         in_pick,
@@ -392,8 +392,7 @@
         out_lines,
         out_core,
         out_back,
-        out_zh_first,
-        lambda k: out_zh[k].second(),
+        out_zh_send,
         out_store,
     )
     for entry in ORDER:
@@ -401,6 +400,14 @@
     comm.drain()
     for store in stores:
         store.wait()
+
+
+def hand_out(*refs):
+    copies = [pltpu.make_async_copy(refs[j], refs[5 + j], refs[10].at[j]) for j in range(5)]
+    for copy in copies:
+        copy.start()
+    for copy in copies:
+        copy.wait()
 
 
 def shards(sizes, pieces, tokens, expert_ids, route_weights, out_grad, gate_weight, up_weight, down_weight):
@@ -428,32 +435,42 @@
         + each(n_y, n_zh, 8, hw)
         + each(3, n_zh, 8, hw)
         + each(n_zh, 8, hw)
-        + each(8, hw)
-        + each(2, 8, hw)
+        + each(3, 8, hw)
         + [
             vm(2 * ff, width), vm(ff, width), vm(2 * ff, width), vm(ff, width),
             vm(2 * SLOTS, lanes), vm(2 * SLOTS, lanes),
             vm(lanes // n_c, n_c * 2 * SLOTS), vm(lanes // n_c, n_c * 2 * SLOTS),
             fl(2 * ff, n_dp * SLOTS), fl(ff, n_dp * SLOTS),
             vm(ff, n_dp * SLOTS), vm(n_dp * SLOTS, ff), vm(2 * ff, n_dp * SLOTS), vm(n_dp * SLOTS, 2 * ff),
+            vm(lanes, lanes), fl(n_c * 2 * SLOTS, lanes), fl(n_c * 2 * SLOTS, lanes),
             pltpu.SemaphoreType.DMA((copies,)), pltpu.SemaphoreType.DMA((copies,)),
             pltpu.SemaphoreType.DMA((3 + 3 * pieces,)),
         ]
     )
     any_space = pl.BlockSpec(memory_space=pl.ANY)
     vmem = pl.BlockSpec(memory_space=pltpu.VMEM)
+    hbm = pl.BlockSpec(memory_space=pltpu.HBM)
     like = lambda a: jax.ShapeDtypeStruct(a.shape, BF16)
-    return pl.pallas_call(
+    held = pl.pallas_call(
         functools.partial(kernel, sizes, pieces),
         out_shape=(like(tokens), like(tokens), like(gate_weight), like(gate_weight), like(gate_weight)),
-        in_specs=[vmem, vmem, vmem, any_space, any_space, any_space],
+        in_specs=[vmem, vmem, vmem, hbm, hbm, hbm],
         out_specs=(vmem, vmem, any_space, any_space, any_space),
         scratch_shapes=scratch,
         compiler_params=pltpu.CompilerParams(
-            collective_id=0, has_side_effects=True, vmem_limit_bytes=56 * 2**20
+            collective_id=0, has_side_effects=True, vmem_limit_bytes=51 * 2**20
         ),
         name="experts",
     )(tokens, out_grad, meta, gate_weight, up_weight, down_weight)
+    return pl.pallas_call(
+        hand_out,
+        out_shape=tuple(like(a) for a in held),
+        in_specs=[vmem] * 5,
+        out_specs=[hbm] * 5,
+        scratch_shapes=[pltpu.SemaphoreType.DMA((5,))],
+        compiler_params=pltpu.CompilerParams(vmem_limit_bytes=8 * 2**20),
+        name="results",
+    )(*held)
 
 
 def solution(mesh):

time: 147 us -> 140 us (0.952); the launches traced: 145 us -> 140 us
  local copies, waits for them, and re-layouts: 7.2 us -> 2.28 us
    unnamed x14 -> x7, local copies, waits for them, and re-layouts: 7.1 us -> 2.17 us
where the time goes in v3:
time: 140 us
  Pallas kernels  136 us (97%)
  local copies, waits for them, and re-layouts  2.28 us (2%)
    pallas_call x1, Pallas kernels, shards(): pl.pallas_call(functools.partial(kernel, sizes, pieces), out_shape=(like(...  135 us

profile of v3, /device:TPU:1, one launch (start us, length us, event | category | flops | bytes accessed | tf_op | source)
XLA Modules:
  0.0 139.7 jit_solution(11974445417940362969)
XLA Ops:
  0.6 0.7 convert_element_type.5
  1.3 0.0 copy-start.2
  1.3 0.1 copy.14
  1.4 0.5 copy-done.2
  2.0 0.1 copy.15
  2.1 0.1 fusion.5.meta
  2.2 0.0 copy-start
  2.2 0.8 copy-done
  2.9 0.0 copy-start.1
  2.9 0.8 copy-done.1
  3.7 134.5 %experts.1 = (bf16[4,4096]{1,0:T(4,128)(2,1)S(1)}, bf16[4,4096]{1,0:T(4,128)(2,1)S(1)}, bf16[1,96,4096]{2,1,0:T(8,128)(2,1)S(1)}, bf16[1,96,4096]{2,1,0:T(8,128)(2,1)S(1)}, bf16[1,96,4096]{2,1,0:T(8,128)(2,1)S(1)}) custom-call(bf16[4,4096]{1,0:T(4,128)(2,1)S(1)} %copy-done, bf16[4,4096]{1,0:T(4,128)(2,1)S(1)} %copy-done.1, bf16[8,128]{1,0:T(8,128)(2,1)S(1)} %fusion.5.meta, ...), custom_call_target="tpu_custom_call" | custom-call | tf_op jit(solution)/shard_map/experts/pallas_call | solution.py:454
  138.2 1.5 %results.1 = (bf16[4,4096]{1,0:T(4,128)(2,1)}, bf16[4,4096]{1,0:T(4,128)(2,1)}, bf16[1,96,4096]{2,1,0:T(8,128)(2,1)}, bf16[1,96,4096]{2,1,0:T(8,128)(2,1)}, bf16[1,96,4096]{2,1,0:T(8,128)(2,1)}) custom-call(bf16[4,4096]{1,0:T(4,128)(2,1)S(1)} %get-tuple-element.10.refs_0_, bf16[4,4096]{1,0:T(4,128)(2,1)S(1)} %get-tuple-element.11.refs_1_, ...), custom_call_target="tpu_custom_call" | custom-call | tf_op jit(solution)/shard_map/results/pallas_call | solution.py:465
Async XLA Ops:
  1.3 0.7 copy-start.2
  2.2 0.8 copy-start
  2.9 0.8 copy-start.1

commit v4 on v3

--- a/solution.py
+++ b/solution.py
@@ -91,6 +91,43 @@
         ahead = self.at(self.d)
         self.comm.arrived(self.buf.at[ahead], self.device(ahead), self.sem + 1)
         self.comm.arrived(self.buf.at[self.at(2)], self.device(self.at(-self.d)), self.sem + 2)
+
+
+class LineRing:
+    def __init__(self, comm, buf, index, size, line, lines, device, turn):
+        self.comm, self.buf, self.i, self.n, self.device = comm, buf, index, size, device
+        self.line, self.lines = line, lines
+        self.d = 1 if turn % 2 == 0 else -1
+        self.sem = comm.reserve(2 * lines + 1)
+
+    def at(self, step):
+        return lax.rem(self.i + step + self.n, self.n)
+
+    def near(self, ahead):
+        if self.n == 1:
+            return
+        block = self.buf.at[self.i, lax.rem(self.line + ahead, self.lines)]
+        for j, step in enumerate((self.d, -self.d)):
+            self.comm.start(block, block, self.device(self.at(step)), self.sem + 2 * ahead + j)
+
+    def landed(self, step, j):
+        source = self.at(step)
+        for ahead in range(self.lines):
+            block = self.buf.at[source, lax.rem(self.line + ahead, self.lines)]
+            self.comm.arrived(block, self.device(source), self.sem + 2 * ahead + j)
+
+    def far(self):
+        if self.n == 1:
+            return
+        self.landed(-self.d, 0)
+        back = self.buf.at[self.at(-self.d)]
+        self.comm.start(back, back, self.device(self.at(self.d)), self.sem + 2 * self.lines)
+
+    def finish(self):
+        if self.n == 1:
+            return
+        self.landed(self.d, 1)
+        self.comm.arrived(self.buf.at[self.at(2)], self.device(self.at(-self.d)), self.sem + 2 * self.lines)
 
 
 class Spread:
@@ -218,13 +255,14 @@
         lo = k % pieces * wc
         return slice(lo, lo + wc)
 
+    of_token = ones_where(iota((8, META), 0) % 4 == iota((8, META), 1)).astype(BF16)
     for k in items:
         source, lo = tokens if k < pieces else out_grad, k % pieces * wc
         own = jnp.concatenate(
             [source[:, lo : lo + hw].astype(F32), source[:, lo + hw : lo + wc].astype(F32)], axis=0
         ).astype(BF16)
         if k == 0:
-            got[k][c, y, zh, :, :META] = meta[...]
+            got[k][c, y, zh, :, :META] = nt(of_token, meta[...]).astype(BF16)
             got[k][c, y, zh, :, META:] = own
         else:
             got[k][c, y, zh] = own
@@ -237,7 +275,7 @@
     in_y = [Spread(comm, got[k].at[c], y, n_y, to_y) for k in items]
     in_c = [comm.reserve(1) for k in items]
     in_zl = [Spread(comm, slots[k].at[x], zl, n_zl, to_zl) for k in items]
-    in_x = [RingGather(comm, slots[k], x, n_x, to_x, k) for k in items]
+    in_x = [LineRing(comm, slots[k], x, n_x, zl, n_zl, to_x, k) for k in items]
     out_x = [RingReduce(comm, part[k], x_far[k], x_near[k], x, n_x, to_x, k) for k in items]
     out_zl = [Collect(comm, x_sum[k], z_near[k], zl, n_zl, to_zl) for k in items]
     out_c = [comm.reserve(1) for k in items]
@@ -292,12 +330,14 @@
         slots[k][x, zl, :, :hw] = picked[:SLOTS]
         slots[k][x, zl, :, hw:] = picked[SLOTS:]
         in_zl[k].send()
+        in_x[k].near(0)
         if k == 0:
             turn_pickers()
 
     def in_x_near(k):
         in_zl[k].finish()
-        in_x[k].near()
+        for ahead in range(1, n_zl):
+            in_x[k].near(ahead)
 
     def rows_of(k):
         return slots[k][...].reshape(n_dp * SLOTS, wc)
@@ -417,12 +457,12 @@
     wc = width // pieces
     hw = wc // 2
     lanes = n_ex * 8
-    facts = jnp.concatenate([expert_ids.astype(BF16), route_weights], axis=1)
-    meta = jnp.pad(jnp.concatenate([facts, facts], axis=0), ((0, 0), (0, META - 4)))
+    facts = jnp.concatenate([expert_ids.T.astype(BF16), route_weights.T], axis=0)
+    meta = jnp.pad(facts, ((0, META - 4), (0, META - 4)))
     vm = lambda *shape: pltpu.VMEM(shape, BF16)
     fl = lambda *shape: pltpu.VMEM(shape, F32)
     each = lambda *shape: [vm(*shape) for _ in range(2 * pieces)]
-    copies = 2 * pieces * 26
+    copies = 2 * pieces * (24 + 2 * n_zl)
     scratch = (
         [vm(n_c, n_y, n_zh, 8, hw + (META if k == 0 else 0)) for k in range(2 * pieces)]
         + each(n_x, n_zl, SLOTS, wc)

time: 140 us -> 138 us (0.986)
  Pallas kernels: 136 us -> 134 us
    pallas_call x1, Pallas kernels: 135 us -> 133 us  [shards(): pl.pallas_call(functools.partial(kernel, sizes, pieces), out_shape=(like(...]
where the time goes in v4:
time: 138 us; the launch traced here: 137 us
  Pallas kernels  134 us (97%)
  local copies, waits for them, and re-layouts  1.42 us (1%)
    pallas_call x1, Pallas kernels, shards(): pl.pallas_call(functools.partial(kernel, sizes, pieces), out_shape=(like(...  133 us

profile of v4, /device:TPU:1, one launch (start us, length us, event | category | flops | bytes accessed | tf_op | source)
XLA Modules:
  0.0 137.0 jit_solution(7591041847086464873)
XLA Ops:
  0.6 0.0 copy-start.2
  0.6 0.0 copy-start
  0.7 0.7 copy-done.2
  1.3 0.7 fusion.5.meta
  2.0 0.0 copy-done
  2.0 0.0 copy-start.1
  2.0 0.7 copy-done.1
  2.7 132.8 %experts.1 = (bf16[4,4096]{1,0:T(4,128)(2,1)S(1)}, bf16[4,4096]{1,0:T(4,128)(2,1)S(1)}, bf16[1,96,4096]{2,1,0:T(8,128)(2,1)S(1)}, bf16[1,96,4096]{2,1,0:T(8,128)(2,1)S(1)}, bf16[1,96,4096]{2,1,0:T(8,128)(2,1)S(1)}) custom-call(bf16[4,4096]{1,0:T(4,128)(2,1)S(1)} %copy-done, bf16[4,4096]{1,0:T(4,128)(2,1)S(1)} %copy-done.1, bf16[128,128]{1,0:T(8,128)(2,1)S(1)} %fusion.5.meta, ...), custom_call_target="tpu_custom_call" | custom-call | tf_op jit(solution)/shard_map/experts/pallas_call | solution.py:494
  135.5 1.5 %results.1 = (bf16[4,4096]{1,0:T(4,128)(2,1)}, bf16[4,4096]{1,0:T(4,128)(2,1)}, bf16[1,96,4096]{2,1,0:T(8,128)(2,1)}, bf16[1,96,4096]{2,1,0:T(8,128)(2,1)}, bf16[1,96,4096]{2,1,0:T(8,128)(2,1)}) custom-call(bf16[4,4096]{1,0:T(4,128)(2,1)S(1)} %get-tuple-element.10.refs_0_, bf16[4,4096]{1,0:T(4,128)(2,1)S(1)} %get-tuple-element.11.refs_1_, ...), custom_call_target="tpu_custom_call" | custom-call | tf_op jit(solution)/shard_map/results/pallas_call | solution.py:505
  (1 shorter events, 0.0 us)
Async XLA Ops:
  0.6 0.7 copy-start.2
  0.6 1.3 copy-start
  2.0 0.8 copy-start.1
